TPU v7x, 128 devices: a whole 4x4x4 slice. The times are simulated.
128 devices in a mesh: blk: 8 (over y_lo, z), env: 16 (over y_hi, x, core).
Axes of the slice: x: 4, y: 4 (y_hi: 2, y_lo: 2; y = y_hi * 2 + y_lo), z: 4, core: 2. Of those that a mesh axis runs over, the one named last changes fastest.
Arguments:
- psi: float32 [64, 512, 512], P('blk'), may hold values from -6 to 6
- left_env: float32 [32, 16, 512, 512], P('env', 'blk'), may hold values from -0.25 to 0.25
- right_env: float32 [32, 16, 512, 512], P('env', 'blk'), may hold values from -0.046875 to 0.046875
- source: int32 [64, 32], P('blk', 'env'), may hold values from 0 to 63, as said below
- left_sector: int32 [64, 32], P('blk', 'env'), may hold values from 0 to 15, as said below
- right_sector: int32 [64, 32], P('blk', 'env'), may hold values from 0 to 15, as said below
- live: int32 [64, 32], P('blk', 'env'), may hold values from 0 to 1
Outputs:
- sigma: float32 [64, 512, 512], P('blk', 'env')
Inputs may be any that keep to these rules, and one draw needn't show every extreme that they name: source[b, k] - b taken modulo 64 is -1, 0 or 1; both -1 and 1 occur. left_sector[b, k] // 2 == b // 8. right_sector[b, k] // 2 == b // 8.
All inputs are finite; a program needn't handle non-finite values.
Results may differ from a plain program's by a relative error of at most 0.0001.
Values sent between devices are 32-bit elements; how exact they have to be, the bound alone decides.
A program may use at most 192 MiB of HBM per device.

v0:
```python
import jax
import jax.numpy as jnp
from jax import lax
from jax.sharding import PartitionSpec as P


def with_halo(array, sides, width):
    for axis, dim in sides:
        size, length = (lax.axis_size(axis), array.shape[dim])
        up = [(i, (i + 1) % size) for i in range(size)]
        down = [(j, i) for i, j in up]
        last = lax.slice_in_dim(array, length - width, length, axis=dim)
        first = lax.slice_in_dim(array, 0, width, axis=dim)
        before = lax.ppermute(last, axis, up)
        after = lax.ppermute(first, axis, down)
        array = jnp.concatenate([before, array, after], axis=dim)
    return array


def body(psi, left_env, right_env, source, left_sector, right_sector, live):
    blocks, width, _ = psi.shape
    chans = left_env.shape[0]
    sectors = left_env.shape[1]
    total = blocks * lax.axis_size("blk")
    position = lax.axis_index("blk")
    padded = with_halo(psi, (("blk", 0),), 1)
    local_ids = jnp.arange(blocks, dtype=jnp.int32)[:, None]
    glob_ids = position * blocks + local_ids
    offset = (source - glob_ids + total + 1) % total - 1
    src_local = local_ids + 1 + offset
    left_local = left_sector - position * sectors
    right_local = right_sector - position * sectors
    chan_ids = jnp.broadcast_to(jnp.arange(chans, dtype=jnp.int32)[None, :], (blocks, chans))
    weights = live.astype(jnp.float32)
    left_pick = left_env[chan_ids, left_local]
    middle = padded[src_local]
    right_pick = right_env[chan_ids, right_local]
    inner = jnp.einsum("bkij,bkjm->bkim", left_pick, middle, precision=lax.Precision.HIGHEST)
    partial_sum = jnp.einsum(
        "bkim,bkml,bk->ibl", inner, right_pick, weights, precision=lax.Precision.HIGHEST
    )
    share = lax.psum_scatter(partial_sum, "env", scatter_dimension=0, tiled=True)
    return jnp.transpose(share, (1, 0, 2))


def solution(mesh):
    placed = (
        P("blk", None, None),
        P("env", "blk", None, None),
        P("env", "blk", None, None),
        P("blk", "env"),
        P("blk", "env"),
        P("blk", "env"),
        P("blk", "env"),
    )
    return jax.shard_map(
        body, mesh=mesh, in_specs=placed, out_specs=P("blk", "env", None), check_vma=False
    )
```

profile of v0, /device:TPU:0, one launch (start us, length us, event | category | flops | bytes accessed | tf_op | source)
XLA Modules:
  0.0 233.1 jit_solution(8430023958982765745)
XLA Ops:
  6.5 0.0 reduce-scatter.2.cloned.1.call-start
  6.5 2.7 %fusion.17 = (f32[1,512,512]{2,1,0:T(8,128)}, f32[1,512,512]{2,1,0:T(8,128)S(1)}) fusion(f32[8,512,512]{2,1,0:T(8,128)} %param.7), kind=kLoop, calls=%fused_computation.29 | loop fusion | bytes 4194304 | tf_op jit(solution)/shard_map/slice | solution.py:12
  9.2 2.0 collective-permute-start
  11.2 3.1 %collective-permute-start.1 = (f32[1,512,512]{2,1,0:T(8,128)S(1)}, f32[1,512,512]{2,1,0:T(8,128)S(1)}, u32[]{:S(2)}, u32[]{:S(2)}) collective-permute-start(f32[1,512,512]{2,1,0:T(8,128)S(1)} %get-tuple-element.6), channel_id=1, source_target_pairs={{16,0},{32,16},{48,32},{64,48},{80,64},{96,80},{112,96},{0,112},{1... | collective-permute-start | bytes 3145736 | tf_op jit(solution)/shard_map/ppermute | solution.py:15
  14.4 0.7 compare_select_fusion.1
  15.0 0.1 copy.13
  15.1 0.1 reshape.28
  15.2 0.7 fusion.12
  15.9 0.1 copy.12
  16.0 0.1 reshape.20
  16.1 0.1 copy.15
  16.2 0.1 reshape.34
  16.3 0.7 convert_element_type.3
  16.9 0.1 copy.14
  17.0 10.1 %gather_fusion = f32[16,512,512]{2,1,0:T(8,128)} fusion(f32[2,2,512,512]{3,2,1,0:T(8,128)} %param.8, s32[16]{0:T(128)S(1)} %reshape.20), kind=kCustom, calls=%fused_computation | custom fusion | bytes 33554560 | tf_op jit(solution)/shard_map/gather | solution.py:35
  27.1 10.0 %gather_fusion.2 = f32[16,512,512]{2,1,0:T(8,128)} fusion(f32[2,2,512,512]{3,2,1,0:T(8,128)} %param.9, s32[16]{0:T(128)S(1)} %reshape.34), kind=kCustom, calls=%fused_computation.2 | custom fusion | bytes 33554560 | tf_op jit(solution)/shard_map/gather | solution.py:37
  37.2 0.5 collective-permute-done
  37.7 0.0 collective-permute-done.1
  37.7 8.6 %pad_maximum_fusion = f32[10,512,512]{2,1,0:T(8,128)} fusion(f32[1,512,512]{2,1,0:T(8,128)S(1)} %collective-permute-done.1, f32[8,512,512]{2,1,0:T(8,128)} %param.7, f32[1,512,512]{2,1,0:T(8,128)S(1)} %collective-permute-done), kind=kLoop, calls=%fused_computation.5 | loop fusion | flops 5242880 | bytes 20971520 | tf_op jit(solution)/shard_map/concatenate | solution.py:16
  46.3 12.0 %gather_fusion.1 = f32[16,512,512]{2,1,0:T(8,128)} fusion(f32[10,512,512]{2,1,0:T(8,128)} %pad_maximum_fusion, s32[1024]{0:T(1024)S(1)} %pad_clamp_fusion), kind=kCustom, calls=%fused_computation.1 | custom fusion | bytes 33554496 | tf_op jit(solution)/shard_map/gather | solution.py:36
  58.3 32.8 %fusion.18 = f32[8,2,512,512]{3,2,1,0:T(8,128)S(1)} fusion(f32[8,2,512,512]{3,2,1,0:T(8,128)} %bitcast.24, f32[8,2,512,512]{3,2,1,0:T(8,128)} %bitcast.25), kind=kOutput, calls=%fused_computation.30 | convolution fusion | flops 25769803776 | bytes 50331648 | tf_op jit(solution)/shard_map/bkij,bkjm->bkim/dot_general | solution.py:38
  91.1 31.5 %fusion.3 = f32[512,8,512]{2,0,1:T(8,128)} fusion(f32[8,2,512,512]{3,2,1,0:T(8,128)} %bitcast.26, f32[8,2,512,512]{3,2,1,0:T(8,128)S(1)} %fusion.18, f32[8,2]{1,0:T(8,128)S(1)} %copy.14), kind=kOutput, calls=%fused_computation.7 | convolution fusion | flops 25773998080 | bytes 41943104 | tf_op jit(solution)/shard_map/bkim,bkml,bk->ibl/dot_general | solution.py:39
  122.6 0.0 reduce-scatter.2.cloned.1.call-update
  122.6 103.6 %reduce-scatter.2.cloned.1.call-done = f32[32,8,512]{2,0,1:T(8,128)} async-done(((f32[512,8,512]{2,0,1:T(8,128)}), f32[32,8,512]{2,0,1:T(8,128)}) %reduce-scatter.2.cloned.1.call-update) | async-done | bytes 524304 | tf_op jit(solution)/shard_map/reduce_scatter | solution.py:42
  (2 shorter events, 0.0 us)
Async XLA Ops:
  6.5 219.7 %reduce-scatter.2.cloned.1.call-start = ((), (), s32[]{:S(2)}) async-start(), calls=%async_computation.1 | async-start | bytes 8912896 | tf_op jit(solution)/shard_map/reduce_scatter | solution.py:42
  9.2 28.5 %collective-permute-start = (f32[1,512,512]{2,1,0:T(8,128)}, f32[1,512,512]{2,1,0:T(8,128)S(1)}, u32[]{:S(2)}, u32[]{:S(2)}) collective-permute-start(f32[1,512,512]{2,1,0:T(8,128)} %get-tuple-element.5), channel_id=1, source_target_pairs={{0,16},{16,32},{32,48},{48,64},{64,80},{80,96},{96,112},{112,0},{1... | collective-permute-start | bytes 3145736 | tf_op jit(solution)/shard_map/ppermute | solution.py:14
  11.2 26.5 %collective-permute-start.1 = (f32[1,512,512]{2,1,0:T(8,128)S(1)}, f32[1,512,512]{2,1,0:T(8,128)S(1)}, u32[]{:S(2)}, u32[]{:S(2)}) collective-permute-start(f32[1,512,512]{2,1,0:T(8,128)S(1)} %get-tuple-element.6), channel_id=1, source_target_pairs={{16,0},{32,16},{48,32},{64,48},{80,64},{96,80},{112,96},{0,112},{1... | collective-permute-start | bytes 3145736 | tf_op jit(solution)/shard_map/ppermute | solution.py:15
Sparse Core Ops, SparseCore 0:
  122.7 103.4 reduce-scatter.1
where the time goes:
time: 233 us
  waiting for transfers between devices  104 us (45%)
  matrix products  64.3 us (28%)
  local copies, waits for them, and re-layouts  35.4 us (15%)
  between operations  13.4 us (6%)
  other arithmetic  10.7 us (5%)
  starting transfers between devices  5.14 us (2%)
    reduce_scatter x1, waiting for transfers between devices, body(): lax.psum_scatter(partial_sum, 'env', scatter_dimension=0, tiled=True)  104 us
    dot_general x1, matrix products, body(): jnp.einsum('bkij,bkjm->bkim', left_pick, middle, precision=lax.Precision....  32.8 us
    dot_general x1, matrix products, body(): jnp.einsum('bkim,bkml,bk->ibl', inner, right_pick, weights, precision=lax...  31.5 us
    gather x1, local copies, waits for them, and re-layouts, body(): middle = padded[src_local]  12 us
    gather x1, local copies, waits for them, and re-layouts, body(): left_pick = left_env[chan_ids, left_local]  10.1 us
    gather x1, local copies, waits for them, and re-layouts, body(): right_pick = right_env[chan_ids, right_local]  10 us
    concatenate x1, other arithmetic, with_halo(): array = jnp.concatenate([before, array, after], axis=dim)  8.58 us
  transfers between devices with their start and end apart: 3, of which 2 were waited for; matrix products, arithmetic and copies ran while one was open for 10% of the time, Pallas kernels for 0%

commit v1 on v0

v1 whole, which is shorter than its diff:
```python
import functools

import jax
import jax.numpy as jnp
from jax import lax
from jax.experimental import pallas as pl
from jax.experimental.pallas import tpu as pltpu
from jax.sharding import PartitionSpec as P

MESH = pl.DeviceIdType.MESH
BF16 = jnp.bfloat16
F32 = jnp.float32

WIDTH = 512
BLOCKS = 8
STRIP = 32
HALF = 256
HALO_HI, HALO_LO = 8, 9
ORDER = ((0, 0), (1, 0), (0, 1), (1, 3), (0, 2), (1, 1), (1, 2), (0, 3))
CORE, XA1, XA2, YA, YB, XB1, XB2, KINDS = 0, 1, 3, 5, 6, 7, 9, 11


def split(x):
    hi = x.astype(BF16)
    return hi, (x - hi.astype(F32)).astype(BF16)


def dot3(a_hi, a_lo, b_hi, b_lo):
    dot = functools.partial(jnp.dot, preferred_element_type=F32)
    return dot(a_hi, b_hi) + dot(a_hi, b_lo) + dot(a_lo, b_hi)


def kernel(
    source, left_sector, right_sector, live, psi, left, right, out,
    stage, land, p_hi, p_lo, l_hi, l_lo, r_hi, r_lo, cland, sa, sb, xa1, xa2, ya, yb, xb1, xb2, done,
    psi_sem, left_sem, right_sem, halo_send, halo_recv, pass_send, pass_recv, send, recv, out_sem,
):
    blk, env = lax.axis_index("blk"), lax.axis_index("env")
    core, x, y_hi = env % 2, (env // 2) % 4, env // 8

    def env_at(y, xx, c):
        return (y * 4 + xx) * 2 + c

    sibling = (blk, env_at(y_hi, x, 1 - core))
    x_up = (blk, env_at(y_hi, (x + 1) % 4, core))
    x_down = (blk, env_at(y_hi, (x + 3) % 4, core))
    y_other = (blk, env_at(1 - y_hi, x, core))
    blk_up = ((blk + 1) % 8, env)
    blk_down = ((blk + 7) % 8, env)

    def load(what, src, dst, sem):
        return pltpu.make_async_copy(src, dst, sem)

    def left_load(m):
        return load("l", left.at[m], stage.at[m], left_sem.at[m])

    def right_load(m):
        return load("r", right.at[m], stage.at[4 + m], right_sem.at[m])

    def psi_load(j):
        return load("p", psi.at[j], land.at[j], psi_sem.at[j])

    for m in range(4):
        left_load(m).start()
    for j in (0, 1, 2):
        psi_load(j).start()
    for m in range(4):
        right_load(m).start()
    for j in (7, 3, 4, 5, 6):
        psi_load(j).start()

    barrier = pltpu.get_barrier_semaphore()
    for peer in (sibling, x_up, x_down, y_other, blk_up, blk_down):
        pl.semaphore_signal(barrier, inc=1, device_id=peer, device_id_type=MESH)
    pl.semaphore_wait(barrier, 6)

    def remote(src, dst, s, r, peer):
        return pltpu.make_async_remote_copy(
            src_ref=src, dst_ref=dst, send_sem=s, recv_sem=r, device_id=peer, device_id_type=MESH
        )

    my_half = pl.ds(core * HALF, HALF)

    def halo(n):
        mine, theirs, peer = ((0, HALO_HI, blk_down), (7, HALO_LO, blk_up))[n]
        return remote(
            land.at[mine, my_half], land.at[theirs, my_half], halo_send.at[n], halo_recv.at[n], peer
        )

    def halo_pass(n):
        item = (HALO_HI, HALO_LO)[n]
        return remote(
            land.at[item, my_half], land.at[item, my_half], pass_send.at[n], pass_recv.at[n], sibling
        )

    def convert(j):
        hi, lo = split(land[j])
        p_hi[j] = hi
        p_lo[j] = lo

    def convert_left(m):
        left_load(m).wait()
        for half in range(2):
            for s, (dy, dx) in enumerate(ORDER):
                owner = env_at((y_hi + dy) % 2, (x + dx) % 4, (core + 1 + half) % 2)
                hi, lo = split(stage[m, pl.ds(owner * STRIP, STRIP)])
                rows = pl.ds((half * 8 + s) * STRIP, STRIP)
                l_hi[m, rows] = hi
                l_lo[m, rows] = lo

    def convert_right(m):
        right_load(m).wait()
        hi, lo = split(stage[4 + m])
        r_hi[m] = hi
        r_lo[m] = lo

    for m in range(4):
        convert_left(m)
    psi_load(0).wait()
    halo(0).start()
    convert(0)
    for j in (1, 2):
        psi_load(j).wait()
        convert(j)
    for m in range(4):
        convert_right(m)
    psi_load(7).wait()
    halo(1).start()

    def compute(i):
        b = (i + 1) % 8
        glob = blk * BLOCKS + b
        total = None
        for k in range(2):
            offset = jnp.minimum((source[b, k] - glob + 65) % 64, 2) - 1
            item = b + offset
            item = jnp.where(item < 0, HALO_LO, item)
            lm = left_sector[b, k] % 2 + 2 * k
            rm = right_sector[b, k] % 2 + 2 * k
            weight = live[b, k].astype(F32)
            inner = dot3(l_hi[lm], l_lo[lm], p_hi[item], p_lo[item])
            hi, lo = split(inner * weight)
            term = dot3(hi, lo, r_hi[rm], r_lo[rm])
            total = term if total is None else total + term
        stage[i] = total

    def core_copy(i):
        return remote(
            stage.at[i, pl.ds(0, HALF)], cland.at[i], send.at[i, CORE], recv.at[i, CORE], sibling
        )

    def xa1_copy(i, d):
        return remote(
            sa.at[i, pl.ds(4 + 2 * d, 2)], xa1.at[i, d], send.at[i, XA1 + d], recv.at[i, XA1 + d],
            (x_up, x_down)[d],
        )

    def xa2_copy(i, d):
        return remote(
            sa.at[i, 2 + d], xa2.at[i, d], send.at[i, XA2 + d], recv.at[i, XA2 + d], (x_up, x_down)[d]
        )

    def ya_copy(i):
        return remote(sa.at[i, 1], ya.at[i], send.at[i, YA], recv.at[i, YA], y_other)

    def yb_copy(i):
        return remote(sb.at[i, pl.ds(8, 8)], yb.at[i], send.at[i, YB], recv.at[i, YB], y_other)

    def xb1_copy(i, d):
        return remote(
            sb.at[i, pl.ds(4 + 2 * d, 2)], xb1.at[i, d], send.at[i, XB1 + d], recv.at[i, XB1 + d],
            (x_up, x_down)[d],
        )

    def xb2_copy(i, d):
        return remote(
            sb.at[i, 2 + d], xb2.at[i, d], send.at[i, XB2 + d], recv.at[i, XB2 + d], (x_up, x_down)[d]
        )

    def out_copy(i):
        return pltpu.make_async_copy(done.at[i], out.at[(i + 1) % 8], out_sem.at[i])

    def step1(i):
        core_copy(i).wait_recv()
        for s, (dy, dx) in enumerate(ORDER):
            rows = pl.ds(s * STRIP, STRIP)
            strip = stage[i, pl.ds(HALF + s * STRIP, STRIP)] + cland[i, rows]
            sa[i, s] = strip[:, :HALF]
            for h in range(2):
                where = {(0, 0): 0, (0, 1): 1, (1, 0): 2, (1, 1): 5, (2, 0): 4, (2, 1): 6, (3, 0): 7, (3, 1): 3}
                sb[i, 8 * dy + where[dx, h]] = strip[h * 16:(h + 1) * 16, HALF:]
        yb_copy(i).start()
        xa1_copy(i, 0).start()
        xa1_copy(i, 1).start()

    def step2(i):
        for d in range(2):
            xa1_copy(i, d).wait_recv()
            sa[i, 2 + d] += xa1[i, d, 0]
            xa2_copy(i, d).start()
        yb_copy(i).wait_recv()
        sb[i, pl.ds(0, 8)] += yb[i]
        xb1_copy(i, 0).start()
        xb1_copy(i, 1).start()

    def step3(i):
        for d in range(2):
            xa2_copy(i, d).wait_recv()
        sa[i, 1] += xa1[i, 0, 1] + xa2[i, 1]
        ya_copy(i).start()
        for d in range(2):
            xb1_copy(i, d).wait_recv()
            sb[i, 2 + d] += xb1[i, d, 0]
            xb2_copy(i, d).start()

    def step4(i):
        for d in range(2):
            xb2_copy(i, d).wait_recv()
        done[i, pl.ds(0, 16), pl.ds(HALF, HALF)] = sb[i, 0] + xb2[i, 0] + xb1[i, 1, 1]
        done[i, pl.ds(16, 16), pl.ds(HALF, HALF)] = sb[i, 1] + xb1[i, 0, 1] + xb2[i, 1]
        ya_copy(i).wait_recv()
        done[i, :, pl.ds(0, HALF)] = (sa[i, 0] + xa2[i, 0] + xa1[i, 1, 1]) + ya[i]
        out_copy(i).start()

    steps = (step1, step2, step3, step4)

    def iteration(i, carry):
        item = jnp.minimum(i + 3, 9)

        @pl.when(i < 4)
        def _():
            psi_load(i + 3).wait()

        @pl.when(i == 3)
        def _():
            for n in range(2):
                halo(n).wait_recv()
                halo_pass(n).start()

        @pl.when(i == 5)
        def _():
            halo_pass(0).wait_recv()

        @pl.when(i == 6)
        def _():
            halo_pass(1).wait_recv()

        convert(item)
        compute(i)
        core_copy(i).start()
        for n, step in enumerate(steps):
            @pl.when(i > n)
            def _():
                step(i - 1 - n)
        return carry

    lax.fori_loop(0, BLOCKS, iteration, 0)
    for late in range(4):
        for n, step in enumerate(steps):
            if n >= late:
                step(7 + late - n)

    for n in range(2):
        halo(n).wait_send()
        halo_pass(n).wait_send()

    def finish(i, carry):
        core_copy(i).wait_send()
        for d in range(2):
            xa1_copy(i, d).wait_send()
            xa2_copy(i, d).wait_send()
            xb1_copy(i, d).wait_send()
            xb2_copy(i, d).wait_send()
        ya_copy(i).wait_send()
        yb_copy(i).wait_send()
        out_copy(i).wait()
        return carry

    lax.fori_loop(0, BLOCKS, finish, 0)


def body(psi, left_env, right_env, source, left_sector, right_sector, live):
    vmem = pltpu.VMEM
    dma = pltpu.SemaphoreType.DMA
    square = (WIDTH, WIDTH)
    smem = pl.BlockSpec(memory_space=pltpu.SMEM)
    hbm = pl.BlockSpec(memory_space=pl.ANY)
    return pl.pallas_call(
        kernel,
        out_shape=jax.ShapeDtypeStruct((BLOCKS, STRIP, WIDTH), F32),
        in_specs=[smem] * 4 + [hbm] * 3,
        out_specs=hbm,
        scratch_shapes=[
            vmem((8, *square), F32),
            vmem((10, *square), F32),
            vmem((10, *square), BF16),
            vmem((10, *square), BF16),
            vmem((4, *square), BF16),
            vmem((4, *square), BF16),
            vmem((4, *square), BF16),
            vmem((4, *square), BF16),
            vmem((8, HALF, WIDTH), F32),
            vmem((8, 8, STRIP, HALF), F32),
            vmem((8, 16, 16, HALF), F32),
            vmem((8, 2, 2, STRIP, HALF), F32),
            vmem((8, 2, STRIP, HALF), F32),
            vmem((8, STRIP, HALF), F32),
            vmem((8, 8, 16, HALF), F32),
            vmem((8, 2, 2, 16, HALF), F32),
            vmem((8, 2, 16, HALF), F32),
            vmem((8, STRIP, WIDTH), F32),
            dma((8,)), dma((4,)), dma((4,)),
            dma((2,)), dma((2,)), dma((2,)), dma((2,)),
            dma((8, KINDS)), dma((8, KINDS)), dma((8,)),
        ],
        compiler_params=pltpu.CompilerParams(
            collective_id=0, has_side_effects=True, vmem_limit_bytes=60 * 2**20
        ),
    )(
        source, left_sector, right_sector, live, psi,
        left_env.reshape(4, *square), right_env.reshape(4, *square),
    )


def solution(mesh):
    placed = (
        P("blk", None, None),
        P("env", "blk", None, None),
        P("env", "blk", None, None),
        P("blk", "env"),
        P("blk", "env"),
        P("blk", "env"),
        P("blk", "env"),
    )
    return jax.shard_map(
        body, mesh=mesh, in_specs=placed, out_specs=P("blk", "env", None), check_vma=False
    )
```

time: 233 us -> 72.8 us (0.31)
  waiting for transfers between devices: 104 us -> 0 us
  Pallas kernels: 0 us -> 65.3 us
  matrix products: 64.3 us -> 0 us
  local copies, waits for them, and re-layouts: 35.4 us -> 7.24 us
  between operations: 13.4 us -> 0.01 us
  other arithmetic: 10.7 us -> 0 us
  starting transfers between devices: 5.14 us -> 0 us
    reduce_scatter x1 -> x0, waiting for transfers between devices: 104 us -> none  [body(): lax.psum_scatter(partial_sum, 'env', scatter_dimension=0, tiled=True)]
    pallas_call x0 -> x1, Pallas kernels: none -> 65.3 us  [body(): pl.pallas_call(kernel, out_shape=jax.ShapeDtypeStruct((BLOCKS, STRIP, WID...]
    dot_general x2 -> x0, matrix products: 64.3 us -> none  [the longest x1 32.8 us: body(): jnp.einsum('bkij,bkjm->bkim', left_pick, middle, precision=lax.Precision....]
    gather x3 -> x0, local copies, waits for them, and re-layouts: 32.2 us -> none  [the longest x1 12 us: body(): middle = padded[src_local]]
    concatenate x2 -> x0, other arithmetic: 9.29 us -> none  [the longest x1 8.58 us: with_halo(): array = jnp.concatenate([before, array, after], axis=dim)]
    unnamed x0 -> x5, local copies, waits for them, and re-layouts: none -> 7.24 us
    ppermute x2 -> x0, starting transfers between devices: 5.14 us -> none  [the longest x1 3.14 us: with_halo(): after = lax.ppermute(first, axis, down)]
    slice x1 -> x0, local copies, waits for them, and re-layouts: 2.68 us -> none  [with_halo(): last = lax.slice_in_dim(array, length - width, length, axis=dim)]
  transfers between devices with their start and end apart: 3 -> 0, of which waited for: 2 -> 0; matrix products, arithmetic and copies ran while one was open for 10% -> 0% of each run, Pallas kernels for 0% -> 0%
where the time goes in v1:
time: 72.8 us; the launch traced here: 72.5 us
  Pallas kernels  65.3 us (90%)
  local copies, waits for them, and re-layouts  7.24 us (10%)
    pallas_call x1, Pallas kernels, body(): pl.pallas_call(kernel, out_shape=jax.ShapeDtypeStruct((BLOCKS, STRIP, WID...  65.3 us
    unnamed x5, local copies, waits for them, and re-layouts  7.24 us

profile of v1, /device:TPU:0, one launch (start us, length us, event | category | flops | bytes accessed | tf_op | source)
XLA Modules:
  0.0 72.5 jit_solution(12214325206778469339)
XLA Ops:
  0.0 1.3 %copy.8.source = s32[8,2]{1,0:T(8,128)} copy(s32[8,2]{0,1:T(2,128)} %param.10) | data formatting | bytes 128 | tf_op args[3]
  1.3 1.3 %copy.9.left_sector = s32[8,2]{1,0:T(8,128)} copy(s32[8,2]{0,1:T(2,128)} %param.11) | data formatting | bytes 128 | tf_op args[4]
  2.7 1.3 %copy.10.right_sector = s32[8,2]{1,0:T(8,128)} copy(s32[8,2]{0,1:T(2,128)} %param.12) | data formatting | bytes 128 | tf_op args[5]
  4.0 1.3 %copy.11.live = s32[8,2]{1,0:T(8,128)} copy(s32[8,2]{0,1:T(2,128)} %param.13) | data formatting | bytes 128 | tf_op args[6]
  5.4 65.3 %shard_map.73 = f32[8,32,512]{2,1,0:T(8,128)} custom-call(s32[8,2]{1,0:T(8,128)} %copy.8.source, s32[8,2]{1,0:T(8,128)} %copy.9.left_sector, s32[8,2]{1,0:T(8,128)} %copy.10.right_sector, s32[8,2]{1,0:T(8,128)} %copy.11.live, f32[8,512,512]{2,1,0:T(8,128)} %psi.1, f32[4,512,512]{2,1,0:T(8,128)} %bitcast.2, f32[4,512,512]{2,1,0:T(8,128)} %bitcast.3), custom_call_target="tpu_custom_call" | custom-call | tf_op jit(solution)/shard_map/pallas_call | solution.py:288
  70.7 1.9 %copy.13 = f32[8,32,512]{2,1,0:T(8,128)} copy(f32[8,32,512]{2,1,0:T(8,128)} %shard_map.73) | data formatting | bytes 1048576

commit v2 on v1

--- a/solution.py
+++ b/solution.py
@@ -15,6 +15,9 @@
 BLOCKS = 8
 STRIP = 32
 HALF = 256
+CUT = 384
+REST = WIDTH - CUT
+OFFSETS = (2, 6, 10, 14)
 HALO_HI, HALO_LO = 8, 9
 ORDER = ((0, 0), (1, 0), (0, 1), (1, 3), (0, 2), (1, 1), (1, 2), (0, 3))
 CORE, XA1, XA2, YA, YB, XB1, XB2, KINDS = 0, 1, 3, 5, 6, 7, 9, 11
@@ -32,8 +35,10 @@
 
 def kernel(
     source, left_sector, right_sector, live, psi, left, right, out,
-    stage, land, p_hi, p_lo, l_hi, l_lo, r_hi, r_lo, cland, sa, sb, xa1, xa2, ya, yb, xb1, xb2, done,
-    psi_sem, left_sem, right_sem, halo_send, halo_recv, pass_send, pass_recv, send, recv, out_sem,
+    table, stage, land, p_hi, p_lo, l_hi, l_lo, r_hi, r_lo, i_hi, i_lo,
+    cland, sa, sb, xa1, xa2, ya, yb, xb1, xb2, done,
+    table_sem, psi_sem, left_sem, right_sem, halo_send, halo_recv, pass_send, pass_recv, send, recv,
+    out_sem,
 ):
     blk, env = lax.axis_index("blk"), lax.axis_index("env")
     core, x, y_hi = env % 2, (env // 2) % 4, env // 8
@@ -48,22 +53,27 @@
     blk_up = ((blk + 1) % 8, env)
     blk_down = ((blk + 7) % 8, env)
 
-    def load(what, src, dst, sem):
-        return pltpu.make_async_copy(src, dst, sem)
-
     def left_load(m):
-        return load("l", left.at[m], stage.at[m], left_sem.at[m])
+        return pltpu.make_async_copy(left.at[m], stage.at[m], left_sem.at[m])
 
     def right_load(m):
-        return load("r", right.at[m], stage.at[4 + m], right_sem.at[m])
+        return pltpu.make_async_copy(right.at[m], stage.at[4 + m], right_sem.at[m])
 
     def psi_load(j):
-        return load("p", psi.at[j], land.at[j], psi_sem.at[j])
-
-    for m in range(4):
+        return pltpu.make_async_copy(psi.at[j], land.at[j], psi_sem.at[j])
+
+    table_loads = [
+        pltpu.make_async_copy(ref, table.at[n], table_sem.at[n])
+        for n, ref in enumerate((source, left_sector, right_sector, live))
+    ]
+    for copy in table_loads:
+        copy.start()
+    for m in (0, 1):
         left_load(m).start()
     for j in (0, 1, 2):
         psi_load(j).start()
+    for m in (2, 3):
+        left_load(m).start()
     for m in range(4):
         right_load(m).start()
     for j in (7, 3, 4, 5, 6):
@@ -72,7 +82,6 @@
     barrier = pltpu.get_barrier_semaphore()
     for peer in (sibling, x_up, x_down, y_other, blk_up, blk_down):
         pl.semaphore_signal(barrier, inc=1, device_id=peer, device_id_type=MESH)
-    pl.semaphore_wait(barrier, 6)
 
     def remote(src, dst, s, r, peer):
         return pltpu.make_async_remote_copy(
@@ -84,7 +93,7 @@
     def halo(n):
         mine, theirs, peer = ((0, HALO_HI, blk_down), (7, HALO_LO, blk_up))[n]
         return remote(
-            land.at[mine, my_half], land.at[theirs, my_half], halo_send.at[n], halo_recv.at[n], peer
+            psi.at[mine, my_half], land.at[theirs, my_half], halo_send.at[n], halo_recv.at[n], peer
         )
 
     def halo_pass(n):
@@ -114,33 +123,24 @@
         r_hi[m] = hi
         r_lo[m] = lo
 
-    for m in range(4):
-        convert_left(m)
-    psi_load(0).wait()
-    halo(0).start()
-    convert(0)
-    for j in (1, 2):
-        psi_load(j).wait()
-        convert(j)
-    for m in range(4):
-        convert_right(m)
-    psi_load(7).wait()
-    halo(1).start()
-
-    def compute(i):
+    def first(i, k):
         b = (i + 1) % 8
-        glob = blk * BLOCKS + b
+        offset = jnp.minimum((table[0, k, b] - (blk * BLOCKS + b) + 65) % 64, 2) - 1
+        item = b + offset
+        item = jnp.where(item < 0, HALO_LO, item)
+        lm = table[1, k, b] % 2 + 2 * k
+        weight = table[3, k, b].astype(F32)
+        inner = dot3(l_hi[lm], l_lo[lm], p_hi[item], p_lo[item])
+        hi, lo = split(inner * weight)
+        i_hi[k] = hi
+        i_lo[k] = lo
+
+    def second(i):
+        b = (i + 1) % 8
         total = None
         for k in range(2):
-            offset = jnp.minimum((source[b, k] - glob + 65) % 64, 2) - 1
-            item = b + offset
-            item = jnp.where(item < 0, HALO_LO, item)
-            lm = left_sector[b, k] % 2 + 2 * k
-            rm = right_sector[b, k] % 2 + 2 * k
-            weight = live[b, k].astype(F32)
-            inner = dot3(l_hi[lm], l_lo[lm], p_hi[item], p_lo[item])
-            hi, lo = split(inner * weight)
-            term = dot3(hi, lo, r_hi[rm], r_lo[rm])
+            rm = table[2, k, b] % 2 + 2 * k
+            term = dot3(i_hi[k], i_lo[k], r_hi[rm], r_lo[rm])
             total = term if total is None else total + term
         stage[i] = total
 
@@ -185,10 +185,10 @@
         for s, (dy, dx) in enumerate(ORDER):
             rows = pl.ds(s * STRIP, STRIP)
             strip = stage[i, pl.ds(HALF + s * STRIP, STRIP)] + cland[i, rows]
-            sa[i, s] = strip[:, :HALF]
+            sa[i, s] = strip[:, :CUT]
             for h in range(2):
                 where = {(0, 0): 0, (0, 1): 1, (1, 0): 2, (1, 1): 5, (2, 0): 4, (2, 1): 6, (3, 0): 7, (3, 1): 3}
-                sb[i, 8 * dy + where[dx, h]] = strip[h * 16:(h + 1) * 16, HALF:]
+                sb[i, 8 * dy + where[dx, h]] = strip[h * 16:(h + 1) * 16, CUT:]
         yb_copy(i).start()
         xa1_copy(i, 0).start()
         xa1_copy(i, 1).start()
@@ -216,27 +216,65 @@
     def step4(i):
         for d in range(2):
             xb2_copy(i, d).wait_recv()
-        done[i, pl.ds(0, 16), pl.ds(HALF, HALF)] = sb[i, 0] + xb2[i, 0] + xb1[i, 1, 1]
-        done[i, pl.ds(16, 16), pl.ds(HALF, HALF)] = sb[i, 1] + xb1[i, 0, 1] + xb2[i, 1]
+        done[i, pl.ds(0, 16), pl.ds(CUT, REST)] = sb[i, 0] + xb2[i, 0] + xb1[i, 1, 1]
+        done[i, pl.ds(16, 16), pl.ds(CUT, REST)] = sb[i, 1] + xb1[i, 0, 1] + xb2[i, 1]
         ya_copy(i).wait_recv()
-        done[i, :, pl.ds(0, HALF)] = (sa[i, 0] + xa2[i, 0] + xa1[i, 1, 1]) + ya[i]
+        done[i, :, pl.ds(0, CUT)] = (sa[i, 0] + xa2[i, 0] + xa1[i, 1, 1]) + ya[i]
         out_copy(i).start()
 
     steps = (step1, step2, step3, step4)
 
+    def run_steps(i, slot):
+        for step, offset in zip(steps, OFFSETS):
+            if offset % 2 == slot:
+                ago = offset // 2
+                if isinstance(i, int):
+                    if i >= ago:
+                        step(i - ago)
+                else:
+                    @pl.when(i >= ago)
+                    def _():
+                        step(i - ago)
+
+    for copy in table_loads:
+        copy.wait()
+    convert_left(0)
+    convert_left(1)
+    for j in (0, 1, 2):
+        psi_load(j).wait()
+        convert(j)
+    first(0, 0)
+    convert_left(2)
+    convert_left(3)
+    first(0, 1)
+    pl.semaphore_wait(barrier, 6)
+    halo(0).start()
+    halo(1).start()
+    for m in range(4):
+        convert_right(m)
+    second(0)
+    core_copy(0).start()
+    psi_load(3).wait()
+    convert(3)
+
     def iteration(i, carry):
-        item = jnp.minimum(i + 3, 9)
-
-        @pl.when(i < 4)
-        def _():
-            psi_load(i + 3).wait()
-
-        @pl.when(i == 3)
+        first(i, 0)
+        first(i, 1)
+        run_steps(i, 0)
+
+        @pl.when(i == 4)
         def _():
             for n in range(2):
                 halo(n).wait_recv()
                 halo_pass(n).start()
 
+        second(i)
+        core_copy(i).start()
+
+        @pl.when(i < 5)
+        def _():
+            psi_load(i + 3).wait()
+
         @pl.when(i == 5)
         def _():
             halo_pass(0).wait_recv()
@@ -245,20 +283,14 @@
         def _():
             halo_pass(1).wait_recv()
 
-        convert(item)
-        compute(i)
-        core_copy(i).start()
-        for n, step in enumerate(steps):
-            @pl.when(i > n)
-            def _():
-                step(i - 1 - n)
+        convert(jnp.minimum(i + 3, 9))
+        run_steps(i, 1)
         return carry
 
-    lax.fori_loop(0, BLOCKS, iteration, 0)
-    for late in range(4):
-        for n, step in enumerate(steps):
-            if n >= late:
-                step(7 + late - n)
+    lax.fori_loop(1, BLOCKS, iteration, 0)
+    late = [(2 * i + off, n, i) for i in range(BLOCKS) for n, off in enumerate(OFFSETS) if 2 * i + off > 15]
+    for _, n, i in sorted(late):
+        steps[n](i)
 
     for n in range(2):
         halo(n).wait_send()
@@ -283,14 +315,14 @@
     vmem = pltpu.VMEM
     dma = pltpu.SemaphoreType.DMA
     square = (WIDTH, WIDTH)
-    smem = pl.BlockSpec(memory_space=pltpu.SMEM)
     hbm = pl.BlockSpec(memory_space=pl.ANY)
     return pl.pallas_call(
         kernel,
         out_shape=jax.ShapeDtypeStruct((BLOCKS, STRIP, WIDTH), F32),
-        in_specs=[smem] * 4 + [hbm] * 3,
+        in_specs=[hbm] * 7,
         out_specs=hbm,
         scratch_shapes=[
+            pltpu.SMEM((4, 2, BLOCKS), jnp.int32),
             vmem((8, *square), F32),
             vmem((10, *square), F32),
             vmem((10, *square), BF16),
@@ -299,25 +331,28 @@
             vmem((4, *square), BF16),
             vmem((4, *square), BF16),
             vmem((4, *square), BF16),
+            vmem((2, *square), BF16),
+            vmem((2, *square), BF16),
             vmem((8, HALF, WIDTH), F32),
-            vmem((8, 8, STRIP, HALF), F32),
-            vmem((8, 16, 16, HALF), F32),
-            vmem((8, 2, 2, STRIP, HALF), F32),
-            vmem((8, 2, STRIP, HALF), F32),
-            vmem((8, STRIP, HALF), F32),
-            vmem((8, 8, 16, HALF), F32),
-            vmem((8, 2, 2, 16, HALF), F32),
-            vmem((8, 2, 16, HALF), F32),
+            vmem((8, 8, STRIP, CUT), F32),
+            vmem((8, 16, 16, REST), F32),
+            vmem((8, 2, 2, STRIP, CUT), F32),
+            vmem((8, 2, STRIP, CUT), F32),
+            vmem((8, STRIP, CUT), F32),
+            vmem((8, 8, 16, REST), F32),
+            vmem((8, 2, 2, 16, REST), F32),
+            vmem((8, 2, 16, REST), F32),
             vmem((8, STRIP, WIDTH), F32),
-            dma((8,)), dma((4,)), dma((4,)),
+            dma((4,)), dma((8,)), dma((4,)), dma((4,)),
             dma((2,)), dma((2,)), dma((2,)), dma((2,)),
-            dma((8, KINDS)), dma((8, KINDS)), dma((8,)),
+            dma((8, KINDS)), dma((8, KINDS)),
+            dma((8,)),
         ],
         compiler_params=pltpu.CompilerParams(
             collective_id=0, has_side_effects=True, vmem_limit_bytes=60 * 2**20
         ),
     )(
-        source, left_sector, right_sector, live, psi,
+        source.T, left_sector.T, right_sector.T, live.T, psi,
         left_env.reshape(4, *square), right_env.reshape(4, *square),
     )
 

time: 72.8 us -> 59.4 us (0.82)
  Pallas kernels: 65.3 us -> 57.3 us
  local copies, waits for them, and re-layouts: 7.24 us -> 1.87 us
    pallas_call x1, Pallas kernels: 65.3 us -> 57.3 us  [body(): pl.pallas_call(kernel, out_shape=jax.ShapeDtypeStruct((BLOCKS, STRIP, WID...]
    unnamed x5 -> x1, local copies, waits for them, and re-layouts: 7.24 us -> 1.87 us
where the time goes in v2:
time: 59.4 us; the launch traced here: 59.2 us
  Pallas kernels  57.3 us (96%)
  local copies, waits for them, and re-layouts  1.87 us (3%)
    pallas_call x1, Pallas kernels, body(): pl.pallas_call(kernel, out_shape=jax.ShapeDtypeStruct((BLOCKS, STRIP, WID...  57.3 us
    unnamed x1, local copies, waits for them, and re-layouts  1.87 us

profile of v2, /device:TPU:0, one launch (start us, length us, event | category | flops | bytes accessed | tf_op | source)
XLA Modules:
  0.0 59.2 jit_solution(13641569868554471114)
XLA Ops:
  0.0 57.3 %shard_map.73 = f32[8,32,512]{2,1,0:T(8,128)} custom-call(s32[2,8]{1,0:T(2,128)} %bitcast.8, s32[2,8]{1,0:T(2,128)} %bitcast.9, s32[2,8]{1,0:T(2,128)} %bitcast.10, s32[2,8]{1,0:T(2,128)} %bitcast.11, f32[8,512,512]{2,1,0:T(8,128)} %psi.1, f32[4,512,512]{2,1,0:T(8,128)} %bitcast.6, f32[4,512,512]{2,1,0:T(8,128)} %bitcast.7), custom_call_target="tpu_custom_call" | custom-call | tf_op jit(solution)/shard_map/pallas_call | solution.py:319
  57.4 1.9 %copy.9 = f32[8,32,512]{2,1,0:T(8,128)} copy(f32[8,32,512]{2,1,0:T(8,128)} %shard_map.73) | data formatting | bytes 1048576

commit v3 on v2

--- a/solution.py
+++ b/solution.py
@@ -17,7 +17,7 @@
 HALF = 256
 CUT = 384
 REST = WIDTH - CUT
-OFFSETS = (2, 6, 10, 14)
+OFFSETS = (2, 7, 11, 15)
 HALO_HI, HALO_LO = 8, 9
 ORDER = ((0, 0), (1, 0), (0, 1), (1, 3), (0, 2), (1, 1), (1, 2), (0, 3))
 CORE, XA1, XA2, YA, YB, XB1, XB2, KINDS = 0, 1, 3, 5, 6, 7, 9, 11
@@ -262,11 +262,15 @@
         first(i, 1)
         run_steps(i, 0)
 
-        @pl.when(i == 4)
-        def _():
-            for n in range(2):
-                halo(n).wait_recv()
-                halo_pass(n).start()
+        @pl.when(i == 5)
+        def _():
+            halo(0).wait_recv()
+            halo_pass(0).start()
+
+        @pl.when(i == 6)
+        def _():
+            halo(1).wait_recv()
+            halo_pass(1).start()
 
         second(i)
         core_copy(i).start()

time: 59.4 us -> 57.6 us (0.970)
  Pallas kernels: 57.3 us -> 55.5 us
    pallas_call x1, Pallas kernels: 57.3 us -> 55.5 us  [body(): pl.pallas_call(kernel, out_shape=jax.ShapeDtypeStruct((BLOCKS, STRIP, WID...]
where the time goes in v3:
time: 57.6 us; the launch traced here: 57.4 us
  Pallas kernels  55.5 us (96%)
  local copies, waits for them, and re-layouts  1.87 us (3%)
    pallas_call x1, Pallas kernels, body(): pl.pallas_call(kernel, out_shape=jax.ShapeDtypeStruct((BLOCKS, STRIP, WID...  55.5 us
    unnamed x1, local copies, waits for them, and re-layouts  1.87 us

profile of v3, /device:TPU:0, one launch (start us, length us, event | category | flops | bytes accessed | tf_op | source)
XLA Modules:
  0.0 57.4 jit_solution(14460552138027954508)
XLA Ops:
  0.0 55.5 %shard_map.73 = f32[8,32,512]{2,1,0:T(8,128)} custom-call(s32[2,8]{1,0:T(2,128)} %bitcast.8, s32[2,8]{1,0:T(2,128)} %bitcast.9, s32[2,8]{1,0:T(2,128)} %bitcast.10, s32[2,8]{1,0:T(2,128)} %bitcast.11, f32[8,512,512]{2,1,0:T(8,128)} %psi.1, f32[4,512,512]{2,1,0:T(8,128)} %bitcast.6, f32[4,512,512]{2,1,0:T(8,128)} %bitcast.7), custom_call_target="tpu_custom_call" | custom-call | tf_op jit(solution)/shard_map/pallas_call | solution.py:323
  55.5 1.9 %copy.9 = f32[8,32,512]{2,1,0:T(8,128)} copy(f32[8,32,512]{2,1,0:T(8,128)} %shard_map.73) | data formatting | bytes 1048576

commit v4 on v3

--- a/solution.py
+++ b/solution.py
@@ -189,9 +189,9 @@
             for h in range(2):
                 where = {(0, 0): 0, (0, 1): 1, (1, 0): 2, (1, 1): 5, (2, 0): 4, (2, 1): 6, (3, 0): 7, (3, 1): 3}
                 sb[i, 8 * dy + where[dx, h]] = strip[h * 16:(h + 1) * 16, CUT:]
-        yb_copy(i).start()
         xa1_copy(i, 0).start()
         xa1_copy(i, 1).start()
+        yb_copy(i).start()
 
     def step2(i):
         for d in range(2):

time: 57.6 us -> 57.6 us (level)
  no operation moved by 1% of the time
where the time goes in v4:
time: 57.6 us; the launch traced here: 57.4 us
  Pallas kernels  55.5 us (96%)
  local copies, waits for them, and re-layouts  1.87 us (3%)
    pallas_call x1, Pallas kernels, body(): pl.pallas_call(kernel, out_shape=jax.ShapeDtypeStruct((BLOCKS, STRIP, WID...  55.5 us
    unnamed x1, local copies, waits for them, and re-layouts  1.87 us

profile of v4, /device:TPU:0, one launch (start us, length us, event | category | flops | bytes accessed | tf_op | source)
XLA Modules:
  0.0 57.4 jit_solution(1877575777161898486)
XLA Ops:
  0.0 55.5 %shard_map.73 = f32[8,32,512]{2,1,0:T(8,128)} custom-call(s32[2,8]{1,0:T(2,128)} %bitcast.8, s32[2,8]{1,0:T(2,128)} %bitcast.9, s32[2,8]{1,0:T(2,128)} %bitcast.10, s32[2,8]{1,0:T(2,128)} %bitcast.11, f32[8,512,512]{2,1,0:T(8,128)} %psi.1, f32[4,512,512]{2,1,0:T(8,128)} %bitcast.6, f32[4,512,512]{2,1,0:T(8,128)} %bitcast.7), custom_call_target="tpu_custom_call" | custom-call | tf_op jit(solution)/shard_map/pallas_call | solution.py:323
  55.5 1.9 %copy.9 = f32[8,32,512]{2,1,0:T(8,128)} copy(f32[8,32,512]{2,1,0:T(8,128)} %shard_map.73) | data formatting | bytes 1048576
